TPU v7x, 1024 devices: a whole 4x8x16 slice. The times are simulated.
1024 devices in a mesh: seq: 64 (over z, x), head: 16 (over y, core).
Axes of the slice: x: 4, y: 8, z: 16, core: 2. Of those that a mesh axis runs over, the one named last changes fastest.
Arguments:
- vit_query: bfloat16 [16384, 6144], P('seq', 'head'), may hold values from -2.5 to 2.5
- vit_key: bfloat16 [16384, 6144], P('seq', 'head'), may hold values from -2.5 to 2.5
- vit_value: bfloat16 [16384, 6144], P('seq', 'head'), may hold values from -20 to 20
- image_proj: bfloat16 [6144, 8192], P(None, 'head'), may hold values from -2 to 2
- image_slot: int32 [64], replicated, may hold values from 0 to 63, each once
- image_offset: int32 [64], replicated, may hold values from 0 to 256
- text_embed: bfloat16 [512, 64, 8192], P(None, 'seq', 'head'), may hold values from -36 to 36
- norm_gain: float32 [8192], P('head'), may hold values from 0.1 to 1.9
- kv_weight: bfloat16 [8192, 512], P('head'), may hold values from -0.0625 to 0.0625
Outputs:
- merged: bfloat16 [512, 64, 8192], P(None, 'seq', 'head')
- keys_values: bfloat16 [512, 64, 512], P(None, 'seq')
Inputs may be any that keep to these rules, and one draw needn't show every extreme that they name: `image_slot`: each of the 64 examples holds exactly one image.
All inputs are finite; a program needn't handle non-finite values.
Results may differ from a plain program's by a relative error of at most 0.0061.
Values may be sent and summed in bfloat16 or wider, within the bound.
A program may use at most 32 MiB of HBM per device.

v0:
```python
import math

import jax
import jax.numpy as jnp
from jax import lax
from jax.sharding import PartitionSpec as P

D = 8192
VIT_HD = 128
KV_HD = 256
IMG_TOK = 256
EXAMPLE_LEN = 512


def rotate(key_part, positions):
    half_dim = KV_HD // 2
    exponent = jnp.arange(half_dim, dtype=jnp.float32) * (2.0 / KV_HD)
    frequency = jnp.power(jnp.float32(10000.0), -exponent)
    angles = positions.astype(jnp.float32)[:, None] * frequency[None, :]
    cosine = jnp.cos(angles)
    sine_of = jnp.sin(angles)
    first_half = key_part[:, :half_dim]
    second_half = key_part[:, half_dim:]
    return jnp.concatenate(
        [first_half * cosine - second_half * sine_of, second_half * cosine + first_half * sine_of],
        axis=1,
    )


def finish(summed_kv, total_squares, positions):
    inverse = 1.0 / jnp.sqrt(total_squares / D + 1e-06)
    projected = summed_kv * inverse[:, None]
    rotated = rotate(projected[:, :KV_HD], positions)
    return jnp.concatenate([rotated, projected[:, KV_HD:]], axis=1).astype(jnp.bfloat16)


def encode(vit_query, vit_key, vit_value):
    row_count, local_width = vit_query.shape
    shaped = (row_count // IMG_TOK, IMG_TOK, local_width // VIT_HD, VIT_HD)
    scores = jnp.einsum(
        "iahd,ibhd->ihab",
        vit_query.reshape(shaped),
        vit_key.reshape(shaped),
        preferred_element_type=jnp.float32,
    ) / math.sqrt(VIT_HD)
    weights = jnp.exp(scores)
    attention = (weights / jnp.sum(weights, axis=-1, keepdims=True)).astype(jnp.bfloat16)
    mixed_rows = jnp.einsum(
        "ihab,ibhd->iahd", attention, vit_value.reshape(shaped), preferred_element_type=jnp.float32
    )
    return mixed_rows.astype(jnp.bfloat16).reshape(row_count, local_width)


def spread(token_rows, shifts, peer_count):
    image_count = shifts.shape[0]
    blocks = token_rows.reshape(image_count, IMG_TOK // peer_count, peer_count, token_rows.shape[1])
    return jax.vmap(lambda image_block, amount: jnp.roll(image_block, amount, axis=1))(
        blocks, shifts
    )


def on_device(
    vit_query,
    vit_key,
    vit_value,
    image_proj,
    image_slot,
    image_offset,
    text_embed,
    norm_gain,
    kv_weight,
):
    peer_count = lax.axis_size("seq")
    seq_place = lax.axis_index("seq")
    attended = encode(vit_query, vit_key, vit_value)
    image_rows, local_width = attended.shape
    images_here = image_rows // IMG_TOK
    starts = image_slot * EXAMPLE_LEN + image_offset
    own_starts = lax.dynamic_slice_in_dim(starts, seq_place * images_here, images_here)
    shifts = own_starts % peer_count
    out_width = image_proj.shape[1]
    summed = jnp.dot(
        lax.all_gather(attended, "head", axis=1, tiled=True),
        image_proj,
        preferred_element_type=jnp.float32,
    )
    arrived = lax.all_to_all(
        spread(summed.astype(jnp.bfloat16), shifts, peer_count),
        "seq",
        split_axis=2,
        concat_axis=2,
        tiled=True,
    )
    image_tokens = arrived.reshape(image_rows, out_width)
    local_rows = text_embed.shape[0]
    text_rows = text_embed[:, 0, :]
    positions = jnp.arange(local_rows, dtype=jnp.int32) * peer_count + seq_place
    example = positions // EXAMPLE_LEN
    image_count = image_slot.shape[0]
    matches = example[:, None] == image_slot[None, :]
    owner_image = jnp.sum(
        jnp.where(matches, jnp.arange(image_count, dtype=jnp.int32)[None, :], 0), axis=1
    )
    row_start = jnp.sum(jnp.where(matches, starts[None, :], 0), axis=1)
    within = positions - row_start
    is_image = (within >= 0) & (within < IMG_TOK)
    clipped = jnp.clip(within, 0, IMG_TOK - 1)
    source = owner_image // images_here
    local_slot = owner_image % images_here
    per_peer = IMG_TOK // peer_count
    lookup = (local_slot * per_peer + clipped // peer_count) * peer_count + source
    picked = jnp.take(image_tokens, lookup, axis=0)
    merged = jnp.where(is_image[:, None], picked, text_rows)
    widened = merged.astype(jnp.float32)
    squares = jnp.sum(widened * widened, axis=1)
    scaled = (widened * norm_gain[None, :]).astype(jnp.bfloat16)
    partial_kv = jnp.dot(scaled, kv_weight, preferred_element_type=jnp.float32)
    summed_kv, total_squares = lax.psum((partial_kv, squares), "head")
    keys_values = finish(summed_kv, total_squares, positions)
    return (merged[:, None, :], keys_values[:, None, :])


def solution(mesh):
    placed = (
        P("seq", "head"),
        P("seq", "head"),
        P("seq", "head"),
        P(None, "head"),
        P(),
        P(),
        P(None, "seq", "head"),
        P("head"),
        P("head", None),
    )
    return jax.shard_map(
        on_device,
        mesh=mesh,
        in_specs=placed,
        out_specs=(P(None, "seq", "head"), P(None, "seq", None)),
        check_vma=False,
    )
```

profile of v0, /device:TPU:1, one launch (start us, length us, event | category | flops | bytes accessed | tf_op | source)
XLA Modules:
  0.0 245.1 jit_solution(11909038617683362747)
XLA Ops:
  7.2 1.1 copy.30
  8.3 1.1 copy.31
  9.4 1.1 copy.34
  10.5 0.3 fusion
  10.8 1.0 convolution_convert_fusion.1
  11.8 0.7 multiply_add_fusion.1
  12.5 0.6 dynamic_slice.3
  15.0 54.8 %all-gather.2.cloned.1.call-done = bf16[256,6144]{0,1:T(8,128)(2,1)} async-done(((bf16[256,384]{0,1:T(8,128)(2,1)}), bf16[256,6144]{0,1:T(8,128)(2,1)}) %all-gather.2.cloned.1.call-update) | async-done | bytes 3145744 | tf_op jit(solution)/shard_map/all_gather | solution.py:83
  69.8 5.5 %convolution_convert_fusion = bf16[256,512]{1,0:T(8,128)(2,1)S(1)} fusion(bf16[256,6144]{0,1:T(8,128)(2,1)} %all-gather.2.cloned.1.call-done, bf16[6144,512]{1,0:T(8,128)(2,1)} %param.12), kind=kOutput, calls=%fused_computation.5 | convolution fusion | flops 1610743808 | bytes 9699328 | tf_op jit(solution)/shard_map/dot_general | solution.py:82
  75.4 0.2 copy.36
  75.6 1.1 fusion.16
  76.7 16.1 %all-to-all-start = ((bf16[1,4,64,512]{3,1,0,2:T(4,128)(2,1)}), bf16[1,4,64,512]{3,1,0,2:T(4,128)(2,1)S(1)}, u32[]{:S(2)}, u32[]{:S(2)}) async-start(bf16[1,4,64,512]{3,1,0,2:T(4,128)(2,1)} %fusion.16), calls=%async_computation | async-start | bytes 524288 | tf_op jit(solution)/shard_map/all_to_all | solution.py:87
  92.8 0.0 all-reduce.2.cloned.1.call-start
  92.9 0.1 fusion.18
  93.1 20.1 %all-to-all-done = bf16[1,4,64,512]{3,1,0,2:T(4,128)(2,1)S(1)} async-done(((bf16[1,4,64,512]{3,1,0,2:T(4,128)(2,1)}), bf16[1,4,64,512]{3,1,0,2:T(4,128)(2,1)S(1)}, u32[]{:S(2)}, u32[]{:S(2)}) %all-to-all-start) | async-done | bytes 262176 | tf_op jit(solution)/shard_map/all_to_all | solution.py:87
  113.2 2.0 gather_fusion
  115.2 0.4 fusion.2
  115.6 1.5 fusion.3
  117.2 26.0 %psum.15 = f32[512]{0:T(512)S(1)} all-reduce(f32[512]{0:T(512)S(1)} %get-tuple-element.15), channel_id=1, replica_groups=mesh['seq'=64,'head'=16] {'head'}, use_global_device_ids=true, to_apply=%region_5.6 | all-reduce | flops 512 | bytes 4096 | tf_op jit(solution)/shard_map/psum | solution.py:118
  143.2 1.0 fusion.5
  144.2 90.6 %all-reduce.2.cloned.1.call-done = f32[512,512]{1,0:T(8,128)} async-done(((f32[512,512]{1,0:T(8,128)}), f32[512,512]{1,0:T(8,128)}) %all-reduce.2.cloned.1.call-update) | async-done | bytes 1048592 | tf_op jit(solution)/shard_map/psum | solution.py:118
  234.8 1.4 broadcast_multiply_fusion
  236.2 1.2 fusion.21
  237.4 0.8 pad_maximum_fusion
  (20 shorter events, 0.3 us)
Async XLA Ops:
  7.2 108.5 %copy-start = (bf16[512,512]{1,0:T(8,128)(2,1)S(1)}, bf16[512,512]{1,0:T(8,128)(2,1)}, u32[]{:S(2)}) copy-start(bf16[512,512]{1,0:T(8,128)(2,1)} %param.17) | copy-start | bytes 1572868
  7.2 62.6 %all-gather.2.cloned.1.call-start = ((), (), s32[]{:S(2)}) async-start(), calls=%async_computation.1 | async-start | bytes 3342336 | tf_op jit(solution)/shard_map/all_gather | solution.py:83
  15.0 77.8 %copy-start.3 = (s32[64]{0:T(128)S(1)}, s32[64]{0:T(128)}, u32[]{:S(2)}) copy-start(s32[64]{0:T(128)} %param.13) | copy-start | bytes 772
  75.3 39.8 %copy-start.1 = (bf16[512,1,512]{2,0,1:T(8,128)(2,1)S(1)}, bf16[512,1,512]{2,0,1:T(8,128)(2,1)}, u32[]{:S(2)}) copy-start(bf16[512,1,512]{2,0,1:T(8,128)(2,1)} %param.15) | copy-start | bytes 1572868
  75.4 40.3 %copy-start.2 = (f32[512]{0:T(512)S(1)}, f32[512]{0:T(512)}, u32[]{:S(2)}) copy-start(f32[512]{0:T(512)} %param.16) | copy-start | bytes 6148
  76.7 36.4 %all-to-all-start = ((bf16[1,4,64,512]{3,1,0,2:T(4,128)(2,1)}), bf16[1,4,64,512]{3,1,0,2:T(4,128)(2,1)S(1)}, u32[]{:S(2)}, u32[]{:S(2)}) async-start(bf16[1,4,64,512]{3,1,0,2:T(4,128)(2,1)} %fusion.16), calls=%async_computation | async-start | bytes 524288 | tf_op jit(solution)/shard_map/all_to_all | solution.py:87
  92.8 142.0 %all-reduce.2.cloned.1.call-start = ((), (), s32[]{:S(2)}) async-start(), calls=%async_computation.2 | async-start | bytes 2097152 | tf_op jit(solution)/shard_map/psum | solution.py:118
Sparse Core Ops, SparseCore 0:
  11.9 57.8 all-gather.1
  117.3 117.4 all-reduce.1
where the time goes:
time: 245 us
  waiting for transfers between devices  165 us (67%)
  blocking collectives  26 us (11%)
  between operations  16.2 us (7%)
  starting transfers between devices  16.1 us (7%)
  matrix products  8.31 us (3%)
  other arithmetic  6.86 us (3%)
  local copies, waits for them, and re-layouts  6.11 us (2%)
    psum x1, waiting for transfers between devices, on_device(): summed_kv, total_squares = lax.psum((partial_kv, squares), 'head')  90.6 us
    all_gather x1, waiting for transfers between devices, on_device(): lax.all_gather(attended, 'head', axis=1, tiled=True)  54.8 us
    psum x1, blocking collectives, on_device(): summed_kv, total_squares = lax.psum((partial_kv, squares), 'head')  26 us
    all_to_all x1, waiting for transfers between devices, on_device(): lax.all_to_all(spread(summed.astype(jnp.bfloat16), shifts, peer_count), '...  20.1 us
    all_to_all x1, starting transfers between devices, on_device(): lax.all_to_all(spread(summed.astype(jnp.bfloat16), shifts, peer_count), '...  16.1 us
    dot_general x1, matrix products, on_device(): jnp.dot(lax.all_gather(attended, 'head', axis=1, tiled=True), image_proj,...  5.54 us
  transfers between devices with their start and end apart: 3, of which 3 were waited for; matrix products, arithmetic and copies ran while one was open for 1% of the time, Pallas kernels for 0%

commit v1 on v0

v1 whole, which is shorter than its diff:
```python
import functools
import math

import jax
import jax.numpy as jnp
import numpy as np
from jax import lax
from jax.experimental import pallas as pl
from jax.experimental.pallas import tpu as pltpu
from jax.sharding import PartitionSpec as P

KV_HD = 256
VIT_HD = 128
HEADS = 3
FEAT = 512
KV = 512
KEEP = 4
PACK = FEAT // 128 * KEEP
SIDE = KV_HD + 128
MESH = pl.DeviceIdType.MESH
F32 = jnp.float32
BF16 = jnp.bfloat16


def log2(n):
    return n.bit_length() - 1


def dot(a, b):
    return jnp.dot(a, b, preferred_element_type=F32)


def one_hot(hits):
    return jnp.where(hits, 1.0, 0.0).astype(BF16)


def kernel(
    sizes,
    q_hbm, k_hbm, v_hbm, w_hbm, text_hbm, kvw_hbm, gain, slot_s, offset_s,
    slot_row, offset_row, slot_col, offset_col, freq,
    merged_hbm, kv_hbm,
    q_v, k_v, v_v, w_v, text_v, kvw_v, qp, att, acc, pack_m, unpack_m,
    send_b, recv_b, tok, place, pos, trig, halves, sib_b, rs_send, rs_recv, kvfin, merged_v, kv_v, kv_acc,
    load_sem, out_sem, ring_send, ring_recv, sib_send, sib_recv, a2a_send, a2a_recv,
    half_send, half_recv, rs_ssem, rs_rsem, ag_ssem, ag_rsem, fwd_send, fwd_recv,
):
    n_seq, nz, nx, ny, chunks, img_tok, example_len, d_model = sizes
    hops = ny // 2
    rc = img_tok // chunks
    nj = rc // KEEP
    local_rows = example_len * n_seq // n_seq
    per_example = example_len // n_seq
    group_rows = (img_tok, img_tok // 2, img_tok // 2)
    group_base = (0, img_tok, img_tok + img_tok // 2)
    half_chunks = chunks // 2

    me_s = lax.axis_index("seq")
    me_h = lax.axis_index("head")
    y, core = me_h // 2, me_h % 2
    me_z, me_x = me_s // nx, me_s % nx

    def wrap_y(v):
        return lax.rem(v + 2 * ny, ny)

    def on_ring(v):
        return (me_s, wrap_y(v) * 2 + core)

    sibling = (me_s, y * 2 + 1 - core)

    def remote(src, dst, ssem, rsem, to):
        return pltpu.make_async_remote_copy(
            src_ref=src, dst_ref=dst, send_sem=ssem, recv_sem=rsem, device_id=to, device_id_type=MESH
        )

    loads = [(q_hbm, q_v), (k_hbm, k_v), (v_hbm, v_v), (text_hbm, text_v), (kvw_hbm, kvw_v), (w_hbm, w_v)]
    copies = [pltpu.make_async_copy(a, b, load_sem.at[i]) for i, (a, b) in enumerate(loads)]
    for c in copies:
        c.start()

    barrier = pltpu.get_barrier_semaphore()

    @pl.loop(1, n_seq)
    def _(i):
        pl.semaphore_signal(
            barrier, inc=1, device_id=(lax.rem(me_s + i, n_seq), me_h), device_id_type=MESH
        )

    for d in range(1, ny):
        pl.semaphore_signal(barrier, inc=1, device_id=on_ring(y + d), device_id_type=MESH)
    pl.semaphore_signal(barrier, inc=1, device_id=sibling, device_id_type=MESH)

    def peer_of(n, sign):
        j = n >> log2(KEEP)
        m = j >> log2(nx)
        mag = (nz - m) >> 1
        dz = jnp.where((m & 1) == 0, mag, -mag)
        dx = (nx - 1) - (j & (nx - 1))
        return (((me_z + sign * dz) & (nz - 1)) << log2(nx)) + ((me_x + sign * dx) & (nx - 1))

    def first_position(start):
        return start + ((me_s - start) & (n_seq - 1))

    my_start = slot_s[me_s] * example_len + offset_s[me_s]
    n_q = lax.broadcasted_iota(jnp.int32, (img_tok, img_tok), 0)
    col_q = lax.broadcasted_iota(jnp.int32, (img_tok, img_tok), 1)
    token = ((peer_of(n_q, 1) - my_start) & (n_seq - 1)) + n_seq * (n_q & (KEEP - 1))
    order = one_hot(col_q == token)
    side = PACK * nj
    row_p = lax.broadcasted_iota(jnp.int32, (side, side), 0)
    col_p = lax.broadcasted_iota(jnp.int32, (side, side), 1)

    def packed_from(q):
        return ((q >> log2(KEEP)) & (FEAT // 128 - 1)) * rc + (q >> log2(PACK)) * KEEP + (q & (KEEP - 1))

    pack_m[...] = one_hot(col_p == packed_from(row_p))
    unpack_m[...] = one_hot(row_p == packed_from(col_p))

    copies[0].wait()
    qp[...] = dot(order, q_v[...]).astype(BF16)
    copies[1].wait()
    copies[2].wait()

    def attend(r):
        rows = pl.ds(pl.multiple_of(r * rc, rc), rc)
        for h in range(HEADS):
            cols = slice(h * VIT_HD, (h + 1) * VIT_HD)
            scores = lax.dot_general(
                qp[rows, cols], k_v[:, cols], (((1,), (1,)), ((), ())), preferred_element_type=F32
            ) / math.sqrt(VIT_HD)
            weights = jnp.exp(scores)
            attention = (weights / jnp.sum(weights, axis=-1, keepdims=True)).astype(BF16)
            att[r, y, core * HEADS + h] = dot(attention, v_v[:, cols]).astype(BF16)

    mine = pl.ds(core * HEADS, HEADS)

    def ring_copy(r, way, hop):
        origin = wrap_y(y - (hop - 1)) if way == 0 else wrap_y(y + (hop - 1))
        block = att.at[r, origin, mine]
        to = on_ring(y + 1) if way == 0 else on_ring(y - 1)
        return remote(block, block, ring_send.at[r, way, hop - 1], ring_recv.at[r, way, hop - 1], to)

    def ring_arrival(r, way, hop):
        origin = wrap_y(y - hop) if way == 0 else wrap_y(y + hop)
        block = att.at[r, origin, mine]
        return remote(block, block, ring_send.at[r, way, hop - 1], ring_recv.at[r, way, hop - 1], sibling)

    def origin_of(slot):
        return wrap_y(y - slot) if slot <= hops else wrap_y(y + (slot - hops))

    def sib_copy(r, slot):
        block = att.at[r, origin_of(slot), mine]
        return remote(block, block, sib_send.at[r, slot], sib_recv.at[r, slot], sibling)

    def sib_arrival(r, slot):
        block = att.at[r, origin_of(slot), pl.ds((1 - core) * HEADS, HEADS)]
        return remote(block, block, sib_send.at[r, slot], sib_recv.at[r, slot], sibling)

    width = 2 * HEADS * VIT_HD

    def accumulate(r, slot):
        sib_arrival(r, slot).wait_recv()
        o = origin_of(slot)
        lhs = jnp.concatenate([att[r, o, i] for i in range(2 * HEADS)], axis=1)
        acc[r] += dot(lhs, w_v[pl.ds(pl.multiple_of(o * width, width), width), :])

    def farthest_way(r):
        return r % 2

    def far_slot_ops(r, op):
        for way in (0, 1):
            @pl.when(farthest_way(r) == way)
            def _():
                op(way)

    def peer_scalar(j):
        m = j // nx
        mag = (nz - m) // 2
        dz = jnp.where(m % 2 == 0, mag, -mag)
        dx = (nx - 1) - j % nx
        return lax.rem(me_z + dz + nz, nz) * nx + lax.rem(me_x + dx, nx)

    def send_chunk(r):
        stacked = jnp.concatenate(
            [acc[r, :, f * 128:(f + 1) * 128].astype(BF16) for f in range(FEAT // 128)], axis=0
        )
        packed = dot(pack_m[...], stacked).astype(BF16)
        send_b[r] = packed.reshape(nj, PACK, 128)

        @pl.when(r == chunks - 1)
        def _():
            recv_b[chunks - 1, nj - 1] = send_b[chunks - 1, nj - 1]

        @pl.loop(0, nj - jnp.where(r == chunks - 1, 1, 0))
        def _(jj):
            remote(
                send_b.at[r, jj], recv_b.at[r, jj], a2a_send.at[r], a2a_recv.at[r],
                (peer_scalar(r * nj + jj), me_h),
            ).start()

    def a2a_all(r):
        n = nj - 1 if r == chunks - 1 else nj
        return remote(
            send_b.at[r, pl.ds(0, n)], recv_b.at[r, pl.ds(0, n)], a2a_send.at[r], a2a_recv.at[r], sibling
        )

    def take_chunk(r):
        a2a_all(r).wait_recv()
        stacked = dot(unpack_m[...], recv_b[r].reshape(nj * PACK, 128)).astype(BF16)
        tok[r * rc:(r + 1) * rc, :] = jnp.concatenate(
            [stacked[f * rc:(f + 1) * rc] for f in range(FEAT // 128)], axis=1
        )

    def kv_partial(g, rows_in):
        n = group_rows[g]
        widened = rows_in.astype(F32)
        squares = jnp.sum(widened * widened, axis=1, keepdims=True)
        scaled = (widened * gain[...]).astype(BF16)
        sums = dot(scaled, kvw_v[...])
        base = slice(group_base[g], group_base[g] + n)
        for half in (0, 1):
            halves[half, base, :KV_HD] = sums[:, half * KV_HD:(half + 1) * KV_HD]
            halves[half, base, KV_HD:] = jnp.broadcast_to(squares, (n, 128))
        half_copy(g).start()

    def half_copy(g):
        base = pl.ds(group_base[g], group_rows[g])
        return remote(
            halves.at[1 - core, base], sib_b.at[base], half_send.at[g], half_recv.at[g], sibling
        )

    def rs_copy(g, d):
        rr = group_rows[g] // ny
        at = pl.multiple_of(group_base[g] + wrap_y(y + d) * rr, rr)
        at_recv = (group_base[g] // ny) * (ny - 1) + (d - 1) * rr
        return remote(
            rs_send.at[pl.ds(at, rr)], rs_recv.at[pl.ds(at_recv, rr)], rs_ssem.at[g, d - 1], rs_rsem.at[g, d - 1],
            on_ring(y + d),
        )

    def kv_scatter(g):
        half_copy(g).wait_recv()
        n = group_rows[g]
        base = slice(group_base[g], group_base[g] + n)
        chip = halves[core, base, :] + sib_b[base, :]
        squares = chip[:, KV_HD:]
        high = squares.astype(BF16)
        low = (squares - high.astype(F32)).astype(BF16)
        lane = lax.broadcasted_iota(jnp.int32, (n, 128), 1)
        rs_send[base, :KV_HD] = chip[:, :KV_HD].astype(BF16)
        rs_send[base, KV_HD:] = jnp.where(lane < 64, high.astype(F32), low.astype(F32)).astype(BF16)
        for d in range(1, ny):
            rs_copy(g, d).start()

    def own_rows(g):
        rr = group_rows[g] // ny
        return pl.ds(pl.multiple_of(group_base[g] + y * rr, rr), rr)

    def ag_copy(g, d):
        block = kvfin.at[core, own_rows(g)]
        return remote(block, block, ag_ssem.at[g, d - 1], ag_rsem.at[g, d - 1], on_ring(y + d))

    def ag_arrival(g, d):
        rr = group_rows[g] // ny
        at = pl.multiple_of(group_base[g] + wrap_y(y - d) * rr, rr)
        block = kvfin.at[core, pl.ds(at, rr)]
        return remote(block, block, ag_ssem.at[g, d - 1], ag_rsem.at[g, d - 1], sibling)

    def fwd_copy(g):
        block = kvfin.at[core, pl.ds(group_base[g], group_rows[g])]
        return remote(block, block, fwd_send.at[g], fwd_recv.at[g], sibling)

    def fwd_arrival(g):
        block = kvfin.at[1 - core, pl.ds(group_base[g], group_rows[g])]
        return remote(block, block, fwd_send.at[g], fwd_recv.at[g], sibling)

    def kv_finish(g):
        rr = group_rows[g] // ny
        total = rs_send[own_rows(g), :].astype(F32)
        for d in range(1, ny):
            rs_copy(g, d).wait_recv()
            at = (group_base[g] // ny) * (ny - 1) + (d - 1) * rr
            total += rs_recv[at:at + rr, :].astype(F32)
        squares = total[:, KV_HD:KV_HD + 1] + total[:, KV_HD + 64:KV_HD + 65]
        projected = total[:, :KV_HD] * (1.0 / jnp.sqrt(squares / d_model + 1e-06))
        first, second = projected[:, :128], projected[:, 128:]
        tb = group_base[g] // ny
        cosine, sine = trig[0, tb:tb + rr, :], trig[1, tb:tb + rr, :]
        kvfin[core, own_rows(g), :128] = (first * cosine - second * sine).astype(BF16)
        kvfin[core, own_rows(g), 128:] = (second * cosine + first * sine).astype(BF16)
        for d in range(1, ny):
            ag_copy(g, d).start()

    def kv_forward(g):
        for d in range(1, ny):
            ag_arrival(g, d).wait_recv()
        fwd_copy(g).start()

    def kv_place(g):
        fwd_arrival(g).wait_recv()
        n = group_rows[g]
        base = slice(group_base[g], group_base[g] + n)
        hot = one_hot(lax.broadcasted_iota(jnp.int32, (local_rows, n), 0) == place[:, base])
        return dot(hot, jnp.concatenate([kvfin[0, base, :], kvfin[1, base, :]], axis=1))

    def prepare():
        n_lane = lax.broadcasted_iota(jnp.int32, (n_seq, img_tok), 1)
        i_sub = lax.broadcasted_iota(jnp.int32, (n_seq, img_tok), 0)
        start_c = slot_col[...] * example_len + offset_col[...]
        first_c = (first_position(start_c) >> log2(n_seq)).astype(F32)
        keep_l = lax.broadcasted_iota(jnp.int32, (1, img_tok), 1)
        row_i = jnp.sum(jnp.where(i_sub == peer_of(n_lane, -1), first_c, 0.0), axis=0, keepdims=True)
        place[:, img_tok:] = row_i.astype(jnp.int32) + (keep_l & (KEEP - 1))
        row_t = jnp.sum(jnp.where(slot_col[...] == (n_lane >> log2(KEEP)), first_c, 0.0), axis=0, keepdims=True)
        place[:, :img_tok] = text_row(row_t.astype(jnp.int32), keep_l)
        n_sub = lax.broadcasted_iota(jnp.int32, (img_tok, n_seq), 0)
        i_lane = lax.broadcasted_iota(jnp.int32, (img_tok, n_seq), 1)
        start_r = slot_row[...] * example_len + offset_row[...]
        first_r = (first_position(start_r) >> log2(n_seq)).astype(F32)
        keep_s = lax.broadcasted_iota(jnp.int32, (img_tok, 1), 0)
        row_i = jnp.sum(jnp.where(i_lane == peer_of(n_sub, -1), first_r, 0.0), axis=1, keepdims=True)
        row_i = row_i.astype(jnp.int32) + (keep_s & (KEEP - 1))
        row_t = jnp.sum(jnp.where(slot_row[...] == (n_sub >> log2(KEEP)), first_r, 0.0), axis=1, keepdims=True)
        row_t = text_row(row_t.astype(jnp.int32), keep_s)
        pos[:img_tok, :] = row_t
        pos[img_tok:, :] = row_i
        hot = one_hot(lax.broadcasted_iota(jnp.int32, (img_tok, local_rows), 1) == row_t)
        copies[3].wait()
        copies[4].wait()
        kv_partial(0, dot(hot, text_v[...]))
        for g in range(3):
            rr = group_rows[g] // ny
            tb = group_base[g] // ny
            angles = (pos[own_rows(g), :] * n_seq + me_s).astype(F32) * freq[...]
            keys = core == 0
            trig[0, tb:tb + rr, :] = jnp.where(keys, jnp.cos(angles), 1.0)
            trig[1, tb:tb + rr, :] = jnp.where(keys, jnp.sin(angles), 0.0)

    def text_row(first, n):
        e, m = n >> log2(KEEP), n & (KEEP - 1)
        row = e * per_example + m
        return jnp.where(row >= first, row + KEEP, row)

    acc[...] = jnp.zeros_like(acc)
    pl.semaphore_wait(barrier, n_seq - 1 + ny)

    def step(r, s):
        if s == 0:
            attend(r)
            for way in (0, 1):
                if hops > 1:
                    ring_copy(r, way, 1).start()
            if hops == 1:
                far_slot_ops(r, lambda way: ring_copy(r, way, 1).start())
            sib_copy(r, 0).start()
        if 1 <= s < hops:
            for way in (0, 1):
                ring_arrival(r, way, s).wait_recv()
                if s + 1 < hops:
                    ring_copy(r, way, s + 1).start()
                else:
                    @pl.when(farthest_way(r) == way)
                    def _():
                        ring_copy(r, way, s + 1).start()
                sib_copy(r, s if way == 0 else hops + s).start()
        if s == hops:
            far_slot_ops(r, lambda way: ring_arrival(r, way, s).wait_recv())
            sib_copy(r, hops).start()
        if s == 1:
            accumulate(r, 0)
        if 2 <= s <= hops:
            accumulate(r, s - 1)
            accumulate(r, hops + s - 1)
        if s == hops + 1:
            accumulate(r, hops)
            send_chunk(r)

    depth = (hops + 3) // 2
    ticks = chunks + depth - 1

    @pl.loop(0, ticks)
    def _(tt):
        for par in (0, 1):
            for back in reversed(range(depth)):
                s = 2 * back + par
                if s > hops + 1:
                    continue
                r = tt - back

                @pl.when((r >= 0) & (r < chunks))
                def _():
                    step(r, s)

            if par == 0:
                @pl.when(tt == 0)
                def _():
                    prepare()
                    copies[5].wait()

                @pl.when(tt == 1)
                def _():
                    kv_scatter(0)

                @pl.when(tt == 2)
                def _():
                    kv_finish(0)

                @pl.when(tt == ticks - 2)
                def _():
                    kv_forward(0)

    for r in range(half_chunks):
        take_chunk(r)
    kv_partial(1, tok[:img_tok // 2, :])
    kv_acc[...] = kv_place(0)
    kv_scatter(1)
    for r in range(half_chunks, chunks):
        take_chunk(r)
    kv_partial(2, tok[img_tok // 2:, :])
    kv_finish(1)
    hot = one_hot(lax.broadcasted_iota(jnp.int32, (local_rows, img_tok), 0) == place[:, img_tok:])
    kv_scatter(2)
    is_image = jnp.sum(hot.astype(F32), axis=1, keepdims=True)
    merged_v[...] = jnp.where(is_image > 0.5, dot(hot, tok[...]), text_v[...].astype(F32)).astype(BF16)
    merged_out = pltpu.make_async_copy(merged_v, merged_hbm, out_sem.at[0])
    merged_out.start()
    kv_forward(1)
    kv_finish(2)
    kv_acc[...] += kv_place(1)
    kv_forward(2)
    kv_v[...] = (kv_acc[...] + kv_place(2)).astype(BF16)
    kv_out = pltpu.make_async_copy(kv_v, kv_hbm, out_sem.at[1])
    kv_out.start()

    @pl.loop(0, chunks)
    def _(r):
        for way in (0, 1):
            for hop in range(1, hops):
                ring_copy(r, way, hop).wait_send()
        far_slot_ops(r, lambda way: ring_copy(r, way, hops).wait_send())
        for slot in range(2 * hops):
            sib_copy(r, slot).wait_send()

    for r in range(chunks):
        a2a_all(r).wait_send()
    for g in range(3):
        half_copy(g).wait_send()
        for d in range(1, ny):
            rs_copy(g, d).wait_send()
            ag_copy(g, d).wait_send()
        fwd_copy(g).wait_send()
    merged_out.wait()
    kv_out.wait()


def on_device(
    nx,
    vit_query,
    vit_key,
    vit_value,
    image_proj,
    image_slot,
    image_offset,
    text_embed,
    norm_gain,
    kv_weight,
):
    n_seq, n_head = lax.axis_size("seq"), lax.axis_size("head")
    nz, ny = n_seq // nx, n_head // 2
    img_tok, local_rows = vit_query.shape[0], text_embed.shape[0]
    chunks = min(4, nz)
    hops = ny // 2
    d_model = n_head * FEAT
    rows = 2 * img_tok
    nj = img_tok // chunks // KEEP
    exponent = np.arange(KV_HD // 2, dtype=np.float32) * np.float32(2.0 / KV_HD)
    freq = jnp.power(jnp.float32(10000.0), -jnp.asarray(exponent))[None, :]
    sizes = (n_seq, nz, nx, ny, chunks, img_tok, local_rows, d_model)
    hbm = pl.BlockSpec(memory_space=pltpu.HBM)
    vmem = pl.BlockSpec(memory_space=pltpu.VMEM)
    smem = pl.BlockSpec(memory_space=pltpu.SMEM)
    dma = pltpu.SemaphoreType.DMA
    merged, keys_values = pl.pallas_call(
        functools.partial(kernel, sizes),
        out_shape=(
            jax.ShapeDtypeStruct((local_rows, FEAT), BF16),
            jax.ShapeDtypeStruct((local_rows, KV), BF16),
        ),
        in_specs=[hbm] * 6 + [vmem, smem, smem] + [vmem] * 5,
        out_specs=(hbm, hbm),
        scratch_shapes=[
            pltpu.VMEM(vit_query.shape, BF16),
            pltpu.VMEM(vit_query.shape, BF16),
            pltpu.VMEM(vit_query.shape, BF16),
            pltpu.VMEM(image_proj.shape, BF16),
            pltpu.VMEM((local_rows, FEAT), BF16),
            pltpu.VMEM(kv_weight.shape, BF16),
            pltpu.VMEM(vit_query.shape, BF16),
            pltpu.VMEM((chunks, ny, 2 * HEADS, img_tok // chunks, VIT_HD), BF16),
            pltpu.VMEM((chunks, img_tok // chunks, FEAT), F32),
            pltpu.VMEM((PACK * nj, PACK * nj), BF16),
            pltpu.VMEM((PACK * nj, PACK * nj), BF16),
            pltpu.VMEM((chunks, nj, PACK, 128), BF16),
            pltpu.VMEM((chunks, nj, PACK, 128), BF16),
            pltpu.VMEM((img_tok, FEAT), BF16),
            pltpu.VMEM((1, rows), jnp.int32),
            pltpu.VMEM((rows, 1), jnp.int32),
            pltpu.VMEM((2, rows // ny, 128), F32),
            pltpu.VMEM((2, rows, SIDE), F32),
            pltpu.VMEM((rows, SIDE), F32),
            pltpu.VMEM((rows, SIDE), BF16),
            pltpu.VMEM((rows // ny * (ny - 1), SIDE), BF16),
            pltpu.VMEM((2, rows, KV_HD), BF16),
            pltpu.VMEM((local_rows, FEAT), BF16),
            pltpu.VMEM((local_rows, KV), BF16),
            pltpu.VMEM((local_rows, KV), F32),
            dma((6,)),
            dma((2,)),
            dma((chunks, 2, hops)),
            dma((chunks, 2, hops)),
            dma((chunks, 2 * hops)),
            dma((chunks, 2 * hops)),
            dma((chunks,)),
            dma((chunks,)),
            dma((3,)),
            dma((3,)),
            dma((3, ny - 1)),
            dma((3, ny - 1)),
            dma((3, ny - 1)),
            dma((3, ny - 1)),
            dma((3,)),
            dma((3,)),
        ],
        compiler_params=pltpu.CompilerParams(
            collective_id=0, has_side_effects=True, vmem_limit_bytes=48 * 1024 * 1024
        ),
        cost_estimate=pl.CostEstimate(flops=2 * 10**9, bytes_accessed=10**7, transcendentals=200000),
    )(
        vit_query,
        vit_key,
        vit_value,
        image_proj,
        text_embed.reshape(local_rows, FEAT),
        kv_weight,
        norm_gain[None, :],
        image_slot,
        image_offset,
        image_slot[None, :],
        image_offset[None, :],
        image_slot[:, None],
        image_offset[:, None],
        freq,
    )
    return merged[:, None, :], keys_values[:, None, :]


def solution(mesh):
    placed = (
        P("seq", "head"),
        P("seq", "head"),
        P("seq", "head"),
        P(None, "head"),
        P(),
        P(),
        P(None, "seq", "head"),
        P("head"),
        P("head", None),
    )
    return jax.shard_map(
        functools.partial(on_device, 4 if mesh.shape["seq"] % 16 == 0 else 2),
        mesh=mesh,
        in_specs=placed,
        out_specs=(P(None, "seq", "head"), P(None, "seq", None)),
        check_vma=False,
    )
```

time: 245 us -> 103 us (0.42)
  waiting for transfers between devices: 165 us -> 0 us
  Pallas kernels: 0 us -> 91.4 us
  blocking collectives: 26 us -> 0 us
  starting transfers between devices: 16.1 us -> 0 us
  between operations: 16.2 us -> 0.65 us
  matrix products: 8.31 us -> 0 us
  other arithmetic: 6.86 us -> 0 us
  local copies, waits for them, and re-layouts: 6.11 us -> 10.6 us
    pallas_call x0 -> x1, Pallas kernels: none -> 91.4 us  [on_device(): pl.pallas_call(functools.partial(kernel, sizes), out_shape=(jax.ShapeDtyp...]
    psum x1 -> x0, waiting for transfers between devices: 90.6 us -> none  [on_device(): summed_kv, total_squares = lax.psum((partial_kv, squares), 'head')]
    all_gather x1 -> x0, waiting for transfers between devices: 54.8 us -> none  [on_device(): lax.all_gather(attended, 'head', axis=1, tiled=True)]
    psum x1 -> x0, blocking collectives: 26 us -> none  [on_device(): summed_kv, total_squares = lax.psum((partial_kv, squares), 'head')]
    all_to_all x1 -> x0, waiting for transfers between devices: 20.1 us -> none  [on_device(): lax.all_to_all(spread(summed.astype(jnp.bfloat16), shifts, peer_count), '...]
    all_to_all x1 -> x0, starting transfers between devices: 16.1 us -> none  [on_device(): lax.all_to_all(spread(summed.astype(jnp.bfloat16), shifts, peer_count), '...]
    dot_general x4 -> x0, matrix products: 8.31 us -> none  [the longest x1 5.54 us: on_device(): jnp.dot(lax.all_gather(attended, 'head', axis=1, tiled=True), image_proj,...]
    unnamed x11 -> x20, local copies, waits for them, and re-layouts: 3.26 us -> 9.09 us
  transfers between devices with their start and end apart: 3 -> 0, of which waited for: 3 -> 0; matrix products, arithmetic and copies ran while one was open for 1% -> 0% of each run, Pallas kernels for 0% -> 0%
where the time goes in v1:
time: 103 us
  Pallas kernels  91.4 us (89%)
  local copies, waits for them, and re-layouts  10.6 us (10%)
    pallas_call x1, Pallas kernels, on_device(): pl.pallas_call(functools.partial(kernel, sizes), out_shape=(jax.ShapeDtyp...  91.4 us
    unnamed x20, local copies, waits for them, and re-layouts  9.09 us

profile of v1, /device:TPU:1, one launch (start us, length us, event | category | flops | bytes accessed | tf_op | source)
XLA Modules:
  0.0 102.6 jit_solution(13630177340992309209)
XLA Ops:
  0.6 0.7 copy.13.offset_col
  1.4 0.7 copy.12.slot_col
  2.1 0.0 copy-start
  2.1 1.0 %copy-done = bf16[512,1,512]{2,0,1:T(8,128)(2,1)S(1)} copy-done((bf16[512,1,512]{2,0,1:T(8,128)(2,1)S(1)}, bf16[512,1,512]{2,0,1:T(8,128)(2,1)}, u32[]{:S(2)}) %copy-start) | copy-done | bytes 524312
  3.2 0.0 copy-start.1
  3.2 1.0 %copy-done.1 = bf16[512,512]{1,0:T(8,128)(2,1)S(1)} copy-done((bf16[512,512]{1,0:T(8,128)(2,1)S(1)}, bf16[512,512]{1,0:T(8,128)(2,1)}, u32[]{:S(2)}) %copy-start.1) | copy-done | bytes 524312
  4.2 0.0 copy-start.2
  4.2 0.9 copy-done.2
  5.1 0.0 copy-start.3
  5.1 0.9 copy-done.3
  6.1 0.0 copy-start.4
  6.1 0.9 copy-done.4
  7.0 0.0 copy-start.5
  7.0 0.7 copy-done.5
  7.6 0.0 copy-start.6
  7.6 0.7 copy-done.6
  8.3 0.0 copy-start.7
  8.3 0.7 copy-done.7
  9.0 0.0 copy-start.8
  9.0 0.7 copy-done.8
  9.6 91.4 %shard_map.113 = (bf16[512,512]{1,0:T(8,128)(2,1)S(1)}, bf16[512,512]{1,0:T(8,128)(2,1)S(1)}) custom-call(bf16[256,384]{1,0:T(8,128)(2,1)S(1)} %copy-done.2, bf16[256,384]{1,0:T(8,128)(2,1)S(1)} %copy-done.3, bf16[256,384]{1,0:T(8,128)(2,1)S(1)} %copy-done.4, bf16[6144,512]{1,0:T(8,128)(2,1)} %w_hbm.1, bf16[512,512]{1,0:T(8,128)(2,1)S(1)} %bitcast.8, ...), custom_call_target="tpu_custom_call" | custom-call | flops 2000000000 | bytes 10000000 | tf_op jit(solution)/shard_map/pallas_call | solution.py:482
  101.0 0.8 copy.16
  101.8 0.8 copy.17
Async XLA Ops:
  2.1 1.0 %copy-start = (bf16[512,1,512]{2,0,1:T(8,128)(2,1)S(1)}, bf16[512,1,512]{2,0,1:T(8,128)(2,1)}, u32[]{:S(2)}) copy-start(bf16[512,1,512]{2,0,1:T(8,128)(2,1)} %param.16) | copy-start | bytes 1572868
  3.2 1.0 %copy-start.1 = (bf16[512,512]{1,0:T(8,128)(2,1)S(1)}, bf16[512,512]{1,0:T(8,128)(2,1)}, u32[]{:S(2)}) copy-start(bf16[512,512]{1,0:T(8,128)(2,1)} %kvw_hbm.1) | copy-start | bytes 1572868
  4.2 0.9 copy-start.2
  5.1 0.9 copy-start.3
  6.1 0.9 copy-start.4
  7.0 0.7 copy-start.5
  7.6 0.7 copy-start.6
  8.3 0.7 copy-start.7
  9.0 0.7 copy-start.8

commit v2 on v1

v2 whole, which is shorter than its diff:
```python
import functools
import math

import jax
import jax.numpy as jnp
import numpy as np
from jax import lax
from jax.experimental import pallas as pl
from jax.experimental.pallas import tpu as pltpu
from jax.sharding import PartitionSpec as P

KV_HD = 256
VIT_HD = 128
HEADS = 3
FEAT = 512
KV = 512
KEEP = 4
PACK = FEAT // 128 * KEEP
SIDE = KV_HD + 128
MESH = pl.DeviceIdType.MESH
F32 = jnp.float32
BF16 = jnp.bfloat16


def log2(n):
    return n.bit_length() - 1


def dot(a, b):
    return jnp.dot(a, b, preferred_element_type=F32)


def one_hot(hits):
    return jnp.where(hits, 1.0, 0.0).astype(BF16)


def kernel(
    sizes,
    q_hbm, k_hbm, v_hbm, w_hbm, text_hbm, kvw_hbm, gain_hbm, slot_hbm, offset_hbm, freq_hbm,
    merged_hbm, kv_hbm,
    q_v, k_v, v_v, w_v, text_v, kvw_v, gain, slot_row, offset_row, freq, qp, att, acc, pack_m, unpack_m,
    send_b, recv_b, src_tok, tok, place, pos, trig, turn, halves, sib_b, rs_send, rs_recv, kvfin,
    img_half, img_sib, img_rs, img_rr, kvs, kvr, kv_img, merged_v, kv_v, kv_acc,
    load_sem, out_sem, ring_send, ring_recv, sib_send, sib_recv, far_recv, a2a_send, a2a_recv,
    half_send, half_recv, rs_ssem, rs_rsem, ag_ssem, ag_rsem, fwd_send, fwd_recv, kva_send, kva_recv,
):
    n_seq, nz, nx, ny, chunks, img_tok, example_len, d_model = sizes
    hops = ny // 2
    rc = img_tok // chunks
    nj = rc // KEEP
    local_rows = example_len
    per_example = example_len // n_seq
    text_rr = img_tok // ny
    half_rows = 2 * rc // 2
    mine_rows = half_rows // ny

    me_s = lax.axis_index("seq")
    me_h = lax.axis_index("head")
    y, core = me_h // 2, me_h % 2
    me_z, me_x = me_s // nx, me_s % nx

    def wrap_y(v):
        return lax.rem(v + 2 * ny, ny)

    def on_ring(v):
        return (me_s, wrap_y(v) * 2 + core)

    sibling = (me_s, y * 2 + 1 - core)

    def remote(src, dst, ssem, rsem, to):
        return pltpu.make_async_remote_copy(
            src_ref=src, dst_ref=dst, send_sem=ssem, recv_sem=rsem, device_id=to, device_id_type=MESH
        )

    loads = [
        (slot_hbm, slot_row), (offset_hbm, offset_row), (q_hbm, q_v), (k_hbm, k_v), (v_hbm, v_v),
        (gain_hbm, gain), (freq_hbm, freq), (text_hbm, text_v), (kvw_hbm, kvw_v), (w_hbm, w_v),
    ]
    copies = [pltpu.make_async_copy(a, b, load_sem.at[i]) for i, (a, b) in enumerate(loads)]
    for c in copies:
        c.start()

    barrier = pltpu.get_barrier_semaphore()

    @pl.loop(1, n_seq)
    def _(i):
        pl.semaphore_signal(
            barrier, inc=1, device_id=(lax.rem(me_s + i, n_seq), me_h), device_id_type=MESH
        )

    for d in range(1, ny):
        pl.semaphore_signal(barrier, inc=1, device_id=on_ring(y + d), device_id_type=MESH)
    pl.semaphore_signal(barrier, inc=1, device_id=sibling, device_id_type=MESH)

    def peer_of(n, sign):
        j = n >> log2(KEEP)
        m = j >> log2(nx)
        mag = (nz - m) >> 1
        dz = jnp.where((m & 1) == 0, mag, -mag)
        dx = (nx - 1) - (j & (nx - 1))
        return (((me_z + sign * dz) & (nz - 1)) << log2(nx)) + ((me_x + sign * dx) & (nx - 1))

    def first_position(start):
        return start + ((me_s - start) & (n_seq - 1))

    copies[0].wait()
    copies[1].wait()
    start_r = (slot_row[...] * example_len + offset_row[...]).astype(F32)
    lanes = lax.broadcasted_iota(jnp.int32, (1, n_seq), 1)
    my_start = jnp.sum(jnp.where(lanes == me_s, start_r, 0.0), axis=1, keepdims=True).astype(jnp.int32)
    n_q = lax.broadcasted_iota(jnp.int32, (img_tok, img_tok), 0)
    col_q = lax.broadcasted_iota(jnp.int32, (img_tok, img_tok), 1)

    def token_of(n):
        return ((peer_of(n, 1) - my_start) & (n_seq - 1)) + n_seq * (n & (KEEP - 1))

    order = one_hot(col_q == token_of(n_q))
    side = PACK * nj
    row_p = lax.broadcasted_iota(jnp.int32, (side, side), 0)
    col_p = lax.broadcasted_iota(jnp.int32, (side, side), 1)

    def packed_from(q):
        return ((q >> log2(KEEP)) & (FEAT // 128 - 1)) * rc + (q >> log2(PACK)) * KEEP + (q & (KEEP - 1))

    pack_m[...] = one_hot(col_p == packed_from(row_p))
    unpack_m[...] = one_hot(row_p == packed_from(col_p))

    copies[2].wait()
    qp[...] = dot(order, q_v[...]).astype(BF16)
    copies[3].wait()
    copies[4].wait()

    def attend(r):
        rows = pl.ds(pl.multiple_of(r * rc, rc), rc)
        for h in range(HEADS):
            cols = slice(h * VIT_HD, (h + 1) * VIT_HD)
            scores = lax.dot_general(
                qp[rows, cols], k_v[:, cols], (((1,), (1,)), ((), ())), preferred_element_type=F32
            ) / math.sqrt(VIT_HD)
            weights = jnp.exp(scores)
            attention = (weights / jnp.sum(weights, axis=-1, keepdims=True)).astype(BF16)
            att[y, core * HEADS + h, rows, :] = dot(attention, v_v[:, cols]).astype(BF16)

    def block_of(r, origin, side_core):
        rows = pl.ds(pl.multiple_of(r * rc, rc), rc)
        return att.at[origin, pl.ds(side_core * HEADS, HEADS), rows]

    def ring_copy(r, way, hop):
        origin = wrap_y(y - (hop - 1)) if way == 0 else wrap_y(y + (hop - 1))
        block = block_of(r, origin, core)
        to = on_ring(y + 1) if way == 0 else on_ring(y - 1)
        return remote(block, block, ring_send.at[way, hop - 1], ring_recv.at[r, way, hop - 1], to)

    def ring_arrival(r, way, hop):
        origin = wrap_y(y - hop) if way == 0 else wrap_y(y + hop)
        block = block_of(r, origin, core)
        return remote(block, block, ring_send.at[way, hop - 1], ring_recv.at[r, way, hop - 1], sibling)

    def origin_of(slot):
        return wrap_y(y - slot) if slot <= hops else wrap_y(y + (slot - hops))

    def sib_recv_sem(r, slot):
        return far_recv.at[r] if slot == hops else sib_recv.at[slot]

    def sib_copy(r, slot):
        block = block_of(r, origin_of(slot), core)
        return remote(block, block, sib_send.at[slot], sib_recv_sem(r, slot), sibling)

    def sib_arrival(r, slot):
        block = block_of(r, origin_of(slot), 1 - core)
        return remote(block, block, sib_send.at[slot], sib_recv_sem(r, slot), sibling)

    def sib_all(slot, side_core):
        block = att.at[origin_of(slot), pl.ds(side_core * HEADS, HEADS)]
        return remote(block, block, sib_send.at[slot], sib_recv.at[slot], sibling)

    width = 2 * HEADS * VIT_HD

    def weights_of(o):
        return w_v[pl.ds(pl.multiple_of(o * width, width), width), :]

    def accumulate(slot, first=False):
        sib_all(slot, 1 - core).wait_recv()
        o = origin_of(slot)
        lhs = jnp.concatenate([att[o, i] for i in range(2 * HEADS)], axis=1)
        product = dot(lhs, weights_of(o))
        if first:
            acc[...] = product
        else:
            acc[...] += product

    def farthest_way(r):
        return r % 2

    def far_slot_ops(r, op):
        for way in (0, 1):
            @pl.when(farthest_way(r) == way)
            def _():
                op(way)

    def peer_scalar(j):
        m = j // nx
        mag = (nz - m) // 2
        dz = jnp.where(m % 2 == 0, mag, -mag)
        dx = (nx - 1) - j % nx
        return lax.rem(me_z + dz + nz, nz) * nx + lax.rem(me_x + dx, nx)

    def send_chunk(r):
        sib_arrival(r, hops).wait_recv()
        o = origin_of(hops)
        rows = pl.ds(pl.multiple_of(r * rc, rc), rc)
        lhs = jnp.concatenate([att[o, i, rows, :] for i in range(2 * HEADS)], axis=1)
        total = (acc[rows, :] + dot(lhs, weights_of(o))).astype(BF16)
        src_tok[rows, :] = total
        stacked = jnp.concatenate(
            [total[:, f * 128:(f + 1) * 128] for f in range(FEAT // 128)], axis=0
        )
        packed = dot(pack_m[...], stacked).astype(BF16)
        send_b[r] = packed.reshape(nj, PACK, 128)

        @pl.when(r == chunks - 1)
        def _():
            recv_b[chunks - 1, nj - 1] = send_b[chunks - 1, nj - 1]

        @pl.loop(0, nj - jnp.where(r == chunks - 1, 1, 0))
        def _(jj):
            remote(
                send_b.at[r, jj], recv_b.at[r, jj], a2a_send.at[r], a2a_recv.at[r],
                (peer_scalar(r * nj + jj), me_h),
            ).start()

    def a2a_all(r):
        n = nj - 1 if r == chunks - 1 else nj
        return remote(
            send_b.at[r, pl.ds(0, n)], recv_b.at[r, pl.ds(0, n)], a2a_send.at[r], a2a_recv.at[r], sibling
        )

    def unpack(blocks):
        stacked = dot(unpack_m[...], blocks).astype(BF16)
        return jnp.concatenate([stacked[f * rc:(f + 1) * rc] for f in range(FEAT // 128)], axis=1)

    def take_chunk(r):
        a2a_all(r).wait_recv()
        tok[r * rc:(r + 1) * rc, :] = unpack(recv_b[r].reshape(nj * PACK, 128))

    def kv_sums(rows_in):
        widened = rows_in.astype(F32)
        squares = jnp.sum(widened * widened, axis=1, keepdims=True)
        return dot((widened * gain[...]).astype(BF16), kvw_v[...]), squares

    def two_parts(squares):
        high = squares.astype(BF16).astype(F32)
        return high, squares - high

    def inverse(squares):
        return 1.0 / jnp.sqrt(squares / d_model + 1e-06)

    def half_copy():
        return remote(halves.at[1 - core], sib_b, half_send.at[0], half_recv.at[0], sibling)

    def text_partial(rows_in):
        sums, squares = kv_sums(rows_in)
        for half in (0, 1):
            halves[half, :, :KV_HD] = sums[:, half * KV_HD:(half + 1) * KV_HD]
            halves[half, :, KV_HD:] = jnp.broadcast_to(squares, (img_tok, 128))
        half_copy().start()

    def text_rs(d):
        at = pl.multiple_of(wrap_y(y + d) * text_rr, text_rr)
        return remote(
            rs_send.at[pl.ds(at, text_rr)], rs_recv.at[pl.ds((d - 1) * text_rr, text_rr)],
            rs_ssem.at[0], rs_rsem.at[0], on_ring(y + d),
        )

    def text_rs_all():
        everything = rs_recv.at[pl.ds(0, (ny - 1) * text_rr)]
        return remote(everything, everything, rs_ssem.at[0], rs_rsem.at[0], sibling)

    def text_scatter():
        half_copy().wait_recv()
        chip = halves[core] + sib_b[...]
        high, low = two_parts(chip[:, KV_HD:])
        lane = lax.broadcasted_iota(jnp.int32, (img_tok, 128), 1)
        rs_send[:, :KV_HD] = chip[:, :KV_HD].astype(BF16)
        rs_send[:, KV_HD:] = jnp.where(lane < 64, high, low).astype(BF16)
        for d in range(1, ny):
            text_rs(d).start()

    def text_rows_of(o):
        return pl.ds(pl.multiple_of(o * text_rr, text_rr), text_rr)

    def text_ag(d):
        block = kvfin.at[core, text_rows_of(y)]
        return remote(block, block, ag_ssem.at[0], ag_rsem.at[0, d - 1], on_ring(y + d))

    def text_ag_arrival(d):
        block = kvfin.at[core, text_rows_of(wrap_y(y - d))]
        return remote(block, block, ag_ssem.at[0], ag_rsem.at[0, d - 1], sibling)

    def text_ag_all():
        block = kvfin.at[core, pl.ds(0, (ny - 1) * text_rr)]
        return remote(block, block, ag_ssem.at[0], ag_rsem.at[0, 0], sibling)

    def text_fwd(side_core):
        block = kvfin.at[side_core]
        return remote(block, block, fwd_send.at[0], fwd_recv.at[0], sibling)

    def text_finish():
        text_rs_all().wait_recv()
        total = rs_send[text_rows_of(y), :].astype(F32)
        for d in range(1, ny):
            total += rs_recv[(d - 1) * text_rr:d * text_rr, :].astype(F32)
        squares = total[:, KV_HD:KV_HD + 1] + total[:, KV_HD + 64:KV_HD + 65]
        projected = total[:, :KV_HD] * inverse(squares)
        first, second = projected[:, :128], projected[:, 128:]
        kvfin[core, text_rows_of(y), :128] = (first * trig[0] - second * trig[1]).astype(BF16)
        kvfin[core, text_rows_of(y), 128:] = (second * trig[0] + first * trig[1]).astype(BF16)
        for d in range(1, ny):
            text_ag(d).start()

    def text_forward():
        for d in range(1, ny):
            text_ag_arrival(d).wait_recv()
        text_fwd(core).start()

    def img_half_copy(g):
        return remote(img_half.at[g, 1 - core], img_sib.at[g], half_send.at[1 + g], half_recv.at[1 + g], sibling)

    def img_partial(g):
        sums, squares = kv_sums(src_tok[pl.ds(pl.multiple_of(g * 2 * rc, 2 * rc), 2 * rc), :])
        for half in (0, 1):
            rows = slice(half * half_rows, (half + 1) * half_rows)
            img_half[g, half, :, :KV] = sums[rows]
            img_half[g, half, :, KV:] = jnp.broadcast_to(squares[rows], (half_rows, 128))
        img_half_copy(g).start()

    def img_scatter(g):
        img_half_copy(g).wait_recv()
        chip = img_half[g, core] + img_sib[g]
        sums = chip[:, :KV].reshape(ny, mine_rows, KV)
        high, low = two_parts(chip[:, KV:].reshape(ny, mine_rows, 128))
        img_rs[g, :, :, :KV_HD] = jnp.concatenate([sums[:, :, :KV_HD], sums[:, :, KV_HD:]], axis=1).astype(BF16)
        img_rs[g, :, :, KV_HD:] = jnp.concatenate([high, low], axis=1).astype(BF16)
        for d in range(1, ny):
            remote(
                img_rs.at[g, wrap_y(y + d)], img_rr.at[g, d - 1], rs_ssem.at[1 + g], rs_rsem.at[1 + g],
                on_ring(y + d),
            ).start()

    def img_rs_all(g):
        return remote(img_rr.at[g], img_rr.at[g], rs_ssem.at[1 + g], rs_rsem.at[1 + g], sibling)

    def img_finish(g):
        img_rs_all(g).wait_recv()
        total = img_rs[g, y].astype(F32)
        for d in range(ny - 1):
            total += img_rr[g, d].astype(F32)
        m = mine_rows
        scale = inverse(total[:m, KV_HD:KV_HD + 1] + total[m:, KV_HD:KV_HD + 1])
        keys, values = total[:m, :KV_HD] * scale, total[m:, :KV_HD] * scale
        first, second = keys[:, :128], keys[:, 128:]
        cosine, sine = turn[g, 0], turn[g, 1]
        parts = (
            first * cosine - second * sine, second * cosine + first * sine, values[:, :128], values[:, 128:],
        )
        swapped = [pltpu.roll(part, KEEP, axis=0) for part in parts]
        lower = lax.broadcasted_iota(jnp.int32, (m, 128), 0) < KEEP
        kvs[g, 0] = jnp.concatenate(
            [jnp.where(lower, parts[0], swapped[1]), jnp.where(lower, parts[2], swapped[3])], axis=0
        ).astype(BF16)
        kvs[g, 1] = jnp.concatenate(
            [jnp.where(lower, swapped[0], parts[1]), jnp.where(lower, swapped[2], parts[3])], axis=0
        ).astype(BF16)
        for one in (0, 1):
            def go():
                j = (2 * g + core) * nj + 2 * y + one
                remote(
                    kvs.at[g, one], kvr.at[core, y, g, one], kva_send.at[g], kva_recv.at[g], (peer_scalar(j), me_h)
                ).start()

            if g == 1 and one == 1:
                pl.when(jnp.logical_not(keeps_own))(go)

                @pl.when(keeps_own)
                def _():
                    kvr[core, y, 1, 1] = kvs[1, 1]
            else:
                go()

    keeps_own = jnp.logical_and(core == 1, y == ny - 1)

    def kva_each(g, wait):
        def all_of(n):
            block = kvr.at[core, y, g, pl.ds(0, n)]
            wait(remote(kvs.at[g, pl.ds(0, n)], block, kva_send.at[g], kva_recv.at[g], sibling))

        if g == 0:
            all_of(2)
        else:
            pl.when(keeps_own)(lambda: all_of(1))
            pl.when(jnp.logical_not(keeps_own))(lambda: all_of(2))

    def img_ag(d):
        return remote(kvr.at[core, y], kvr.at[core, y], ag_ssem.at[1], ag_rsem.at[1, d - 1], on_ring(y + d))

    def img_ag_arrival(d):
        block = kvr.at[core, wrap_y(y - d)]
        return remote(block, block, ag_ssem.at[1], ag_rsem.at[1, d - 1], sibling)

    def img_ag_all():
        block = kvr.at[core, pl.ds(0, ny - 1)]
        return remote(block, block, ag_ssem.at[1], ag_rsem.at[1, 0], sibling)

    def img_fwd(side_core):
        block = kvr.at[side_core]
        return remote(block, block, fwd_send.at[1], fwd_recv.at[1], sibling)

    def prepare():
        n_lane = lax.broadcasted_iota(jnp.int32, (n_seq, img_tok), 1)
        i_sub = lax.broadcasted_iota(jnp.int32, (n_seq, img_tok), 0)
        square_s = lax.broadcasted_iota(jnp.int32, (n_seq, n_seq), 0)
        square_l = lax.broadcasted_iota(jnp.int32, (n_seq, n_seq), 1)

        def column(row):
            return jnp.sum(jnp.where(square_s == square_l, row, 0.0), axis=1, keepdims=True)

        slot_col = column(slot_row[...].astype(F32)).astype(jnp.int32)
        first_r = (first_position(start_r.astype(jnp.int32)) >> log2(n_seq)).astype(F32)
        first_c = column(first_r)
        keep_l = lax.broadcasted_iota(jnp.int32, (1, img_tok), 1)
        row_i = jnp.sum(jnp.where(i_sub == peer_of(n_lane, -1), first_c, 0.0), axis=0, keepdims=True)
        place[:, img_tok:] = row_i.astype(jnp.int32) + (keep_l & (KEEP - 1))
        row_t = jnp.sum(jnp.where(slot_col == (n_lane >> log2(KEEP)), first_c, 0.0), axis=0, keepdims=True)
        place[:, :img_tok] = text_row(row_t.astype(jnp.int32), keep_l)
        n_sub = lax.broadcasted_iota(jnp.int32, (img_tok, n_seq), 0)
        i_lane = lax.broadcasted_iota(jnp.int32, (img_tok, n_seq), 1)
        keep_s = lax.broadcasted_iota(jnp.int32, (img_tok, 1), 0)
        row_t = jnp.sum(jnp.where(slot_row[...] == (n_sub >> log2(KEEP)), first_r, 0.0), axis=1, keepdims=True)
        row_t = text_row(row_t.astype(jnp.int32), keep_s)
        pos[...] = row_t
        hot = one_hot(lax.broadcasted_iota(jnp.int32, (img_tok, local_rows), 1) == row_t)
        for i in range(5, 9):
            copies[i].wait()
        text_partial(dot(hot, text_v[...]))
        keys = core == 0
        angles = (pos[text_rows_of(y), :] * n_seq + me_s).astype(F32) * freq[...]
        trig[0] = jnp.where(keys, jnp.cos(angles), 1.0)
        trig[1] = jnp.where(keys, jnp.sin(angles), 0.0)
        for g in (0, 1):
            n = lax.broadcasted_iota(jnp.int32, (mine_rows, 1), 0)
            n = n + ((2 * g + core) * rc + y * mine_rows)
            angles = (my_start + token_of(n)).astype(F32) * freq[...]
            turn[g, 0] = jnp.cos(angles)
            turn[g, 1] = jnp.sin(angles)

    def text_row(first, n):
        e, m = n >> log2(KEEP), n & (KEEP - 1)
        row = e * per_example + m
        return jnp.where(row >= first, row + KEEP, row)

    pl.semaphore_wait(barrier, n_seq - 1 + ny)

    @pl.loop(0, chunks)
    def _(r):
        attend(r)
        if hops > 1:
            ring_copy(r, 0, 1).start()
            ring_copy(r, 1, 1).start()
        else:
            far_slot_ops(r, lambda way: ring_copy(r, way, 1).start())
        sib_copy(r, 0).start()

    prepare()
    copies[9].wait()

    for hop in range(1, hops):
        @pl.loop(0, chunks)
        def _(r):
            for way in (0, 1):
                ring_arrival(r, way, hop).wait_recv()
                if hop + 1 < hops:
                    ring_copy(r, way, hop + 1).start()
                else:
                    @pl.when(farthest_way(r) == way)
                    def _():
                        ring_copy(r, way, hop + 1).start()
                sib_copy(r, hop if way == 0 else hops + hop).start()

        if hop == 1:
            accumulate(0, first=True)
        else:
            accumulate(hop - 1)
            accumulate(hops + hop - 1)
    text_scatter()
    accumulate(hops - 1)
    accumulate(2 * hops - 1)

    @pl.loop(0, chunks + 1)
    def _(r):
        @pl.when(r < chunks)
        def _():
            far_slot_ops(r, lambda way: ring_arrival(r, way, hops).wait_recv())
            sib_copy(r, hops).start()

        @pl.when(r > 0)
        def _():
            send_chunk(r - 1)

        for g in (0, 1):
            @pl.when(r == 2 * g + 2)
            def _():
                img_partial(g)

    img_scatter(0)
    img_scatter(1)
    text_finish()
    img_finish(0)
    img_finish(1)
    text_forward()
    for r in range(chunks):
        take_chunk(r)
    hot = one_hot(lax.broadcasted_iota(jnp.int32, (local_rows, img_tok), 0) == place[:, img_tok:])
    is_image = jnp.sum(hot.astype(F32), axis=1, keepdims=True)
    for g in (0, 1):
        kva_each(g, lambda c: c.wait_recv())
    for d in range(1, ny):
        img_ag(d).start()
    merged_v[...] = jnp.where(is_image > 0.5, dot(hot, tok[...]), text_v[...].astype(F32)).astype(BF16)
    merged_out = pltpu.make_async_copy(merged_v, merged_hbm, out_sem.at[0])
    merged_out.start()
    text_fwd(1 - core).wait_recv()
    hot_text = one_hot(lax.broadcasted_iota(jnp.int32, (local_rows, img_tok), 0) == place[:, :img_tok])
    kv_acc[...] = dot(hot_text, jnp.concatenate([kvfin[0], kvfin[1]], axis=1))
    for d in range(1, ny):
        img_ag_arrival(d).wait_recv()
    img_fwd(core).start()
    img_fwd(1 - core).wait_recv()
    for r in range(chunks):
        kv_img[r * rc:(r + 1) * rc, :] = unpack(kvr[r % 2, :, r // 2].reshape(nj * PACK, 128))
    kv_v[...] = (kv_acc[...] + dot(hot, kv_img[...])).astype(BF16)
    kv_out = pltpu.make_async_copy(kv_v, kv_hbm, out_sem.at[1])
    kv_out.start()

    for way in (0, 1):
        for hop in range(1, hops + 1):
            n = img_tok if hop < hops else img_tok // 2
            block = att.at[0, pl.ds(0, HEADS), pl.ds(0, n)]
            remote(block, block, ring_send.at[way, hop - 1], ring_recv.at[0, way, hop - 1], sibling).wait_send()
    for slot in range(2 * hops):
        sib_all(slot, core).wait_send()
    for r in range(chunks):
        a2a_all(r).wait_send()
    half_copy().wait_send()
    text_rs_all().wait_send()
    text_ag_all().wait_send()
    text_fwd(core).wait_send()
    for g in (0, 1):
        img_half_copy(g).wait_send()
        img_rs_all(g).wait_send()
        kva_each(g, lambda c: c.wait_send())
    img_ag_all().wait_send()
    img_fwd(core).wait_send()
    merged_out.wait()
    kv_out.wait()


def on_device(
    nx,
    vit_query,
    vit_key,
    vit_value,
    image_proj,
    image_slot,
    image_offset,
    text_embed,
    norm_gain,
    kv_weight,
):
    n_seq, n_head = lax.axis_size("seq"), lax.axis_size("head")
    nz, ny = n_seq // nx, n_head // 2
    img_tok, local_rows = vit_query.shape[0], text_embed.shape[0]
    chunks = min(4, nz)
    hops = ny // 2
    d_model = n_head * FEAT
    rows = 2 * img_tok
    rc = img_tok // chunks
    nj = rc // KEEP
    exponent = np.arange(KV_HD // 2, dtype=np.float32) * np.float32(2.0 / KV_HD)
    freq = jnp.power(jnp.float32(10000.0), -jnp.asarray(exponent))[None, :]
    sizes = (n_seq, nz, nx, ny, chunks, img_tok, local_rows, d_model)
    hbm = pl.BlockSpec(memory_space=pltpu.HBM)
    dma = pltpu.SemaphoreType.DMA
    merged, keys_values = pl.pallas_call(
        functools.partial(kernel, sizes),
        out_shape=(
            jax.ShapeDtypeStruct((local_rows, FEAT), BF16),
            jax.ShapeDtypeStruct((local_rows, KV), BF16),
        ),
        in_specs=[hbm] * 10,
        out_specs=(hbm, hbm),
        scratch_shapes=[
            pltpu.VMEM(vit_query.shape, BF16),
            pltpu.VMEM(vit_query.shape, BF16),
            pltpu.VMEM(vit_query.shape, BF16),
            pltpu.VMEM(image_proj.shape, BF16),
            pltpu.VMEM((local_rows, FEAT), BF16),
            pltpu.VMEM(kv_weight.shape, BF16),
            pltpu.VMEM((1, FEAT), F32),
            pltpu.VMEM((1, n_seq), jnp.int32),
            pltpu.VMEM((1, n_seq), jnp.int32),
            pltpu.VMEM((1, 128), F32),
            pltpu.VMEM(vit_query.shape, BF16),
            pltpu.VMEM((ny, 2 * HEADS, img_tok, VIT_HD), BF16),
            pltpu.VMEM((img_tok, FEAT), F32),
            pltpu.VMEM((PACK * nj, PACK * nj), BF16),
            pltpu.VMEM((PACK * nj, PACK * nj), BF16),
            pltpu.VMEM((chunks, nj, PACK, 128), BF16),
            pltpu.VMEM((chunks, nj, PACK, 128), BF16),
            pltpu.VMEM((img_tok, FEAT), BF16),
            pltpu.VMEM((img_tok, FEAT), BF16),
            pltpu.VMEM((1, rows), jnp.int32),
            pltpu.VMEM((img_tok, 1), jnp.int32),
            pltpu.VMEM((2, img_tok // ny, 128), F32),
            pltpu.VMEM((2, 2, rc // ny, 128), F32),
            pltpu.VMEM((2, img_tok, SIDE), F32),
            pltpu.VMEM((img_tok, SIDE), F32),
            pltpu.VMEM((img_tok, SIDE), BF16),
            pltpu.VMEM((img_tok // ny * (ny - 1), SIDE), BF16),
            pltpu.VMEM((2, img_tok, KV_HD), BF16),
            pltpu.VMEM((2, 2, rc, KV + 128), F32),
            pltpu.VMEM((2, rc, KV + 128), F32),
            pltpu.VMEM((2, ny, 2 * rc // ny, SIDE), BF16),
            pltpu.VMEM((2, ny - 1, 2 * rc // ny, SIDE), BF16),
            pltpu.VMEM((2, 2, PACK, 128), BF16),
            pltpu.VMEM((2, ny, 2, 2, PACK, 128), BF16),
            pltpu.VMEM((img_tok, KV), BF16),
            pltpu.VMEM((local_rows, FEAT), BF16),
            pltpu.VMEM((local_rows, KV), BF16),
            pltpu.VMEM((local_rows, KV), F32),
            dma((10,)),
            dma((2,)),
            dma((2, hops)),
            dma((chunks, 2, hops)),
            dma((2 * hops,)),
            dma((2 * hops,)),
            dma((chunks,)),
            dma((chunks,)),
            dma((chunks,)),
            dma((3,)),
            dma((3,)),
            dma((3,)),
            dma((3,)),
            dma((2,)),
            dma((2, ny - 1)),
            dma((2,)),
            dma((2,)),
            dma((2,)),
            dma((2,)),
        ],
        compiler_params=pltpu.CompilerParams(
            collective_id=0, has_side_effects=True, vmem_limit_bytes=60 * 1024 * 1024
        ),
        cost_estimate=pl.CostEstimate(flops=2 * 10**9, bytes_accessed=10**7, transcendentals=200000),
    )(
        vit_query,
        vit_key,
        vit_value,
        image_proj,
        text_embed.reshape(local_rows, FEAT),
        kv_weight,
        norm_gain[None, :],
        image_slot[None, :],
        image_offset[None, :],
        freq,
    )
    return merged[:, None, :], keys_values[:, None, :]


def solution(mesh):
    placed = (
        P("seq", "head"),
        P("seq", "head"),
        P("seq", "head"),
        P(None, "head"),
        P(),
        P(),
        P(None, "seq", "head"),
        P("head"),
        P("head", None),
    )
    return jax.shard_map(
        functools.partial(on_device, 4 if mesh.shape["seq"] % 16 == 0 else 2),
        mesh=mesh,
        in_specs=placed,
        out_specs=(P(None, "seq", "head"), P(None, "seq", None)),
        check_vma=False,
    )
```

time: 103 us -> 77 us (0.75)
  Pallas kernels: 91.4 us -> 72.4 us
  local copies, waits for them, and re-layouts: 10.6 us -> 3.74 us
    pallas_call x1, Pallas kernels: 91.4 us -> 72.4 us  [on_device(): pl.pallas_call(functools.partial(kernel, sizes), out_shape=(jax.ShapeDtyp...]
    unnamed x20 -> x2, local copies, waits for them, and re-layouts: 9.09 us -> 3.74 us
    broadcast_in_dim x2 -> x0, local copies, waits for them, and re-layouts: 1.49 us -> none  [the longest x1 0.75 us: on_device(): image_offset[:, None]]
where the time goes in v2:
time: 77 us; the launch traced here: 76.8 us
  Pallas kernels  72.4 us (94%)
  local copies, waits for them, and re-layouts  3.74 us (5%)
    pallas_call x1, Pallas kernels, on_device(): pl.pallas_call(functools.partial(kernel, sizes), out_shape=(jax.ShapeDtyp...  72.4 us
    unnamed x2, local copies, waits for them, and re-layouts  3.74 us

profile of v2, /device:TPU:1, one launch (start us, length us, event | category | flops | bytes accessed | tf_op | source)
XLA Modules:
  0.0 76.8 jit_solution(18201563237653427737)
XLA Ops:
  0.6 72.4 %shard_map.113 = (bf16[512,512]{1,0:T(8,128)(2,1)}, bf16[512,512]{1,0:T(8,128)(2,1)}) custom-call(bf16[256,384]{1,0:T(8,128)(2,1)} %q_hbm.1, bf16[256,384]{1,0:T(8,128)(2,1)} %k_hbm.1, bf16[256,384]{1,0:T(8,128)(2,1)} %v_hbm.1, bf16[6144,512]{1,0:T(8,128)(2,1)} %w_hbm.1, bf16[512,512]{1,0:T(8,128)(2,1)} %bitcast.6, bf16[512,512]{1,0:T(8,128)(2,1)} %kvw_hbm.1, ...), custom_call_target="tpu_custom_call" | custom-call | flops 2000000000 | bytes 10000000 | tf_op jit(solution)/shard_map/pallas_call | solution.py:593
  73.0 1.9 %copy.14 = bf16[512,1,512]{2,0,1:T(8,128)(2,1)} copy(bf16[512,1,512]{2,0,1:T(8,128)(2,1)} %bitcast.8) | data formatting | bytes 1048576
  74.9 1.9 %copy.15 = bf16[512,1,512]{2,0,1:T(8,128)(2,1)} copy(bf16[512,1,512]{2,0,1:T(8,128)(2,1)} %bitcast.7) | data formatting | bytes 1048576

commit v3 on v2

--- a/solution.py
+++ b/solution.py
@@ -56,11 +56,13 @@
 
     me_s = lax.axis_index("seq")
     me_h = lax.axis_index("head")
-    y, core = me_h // 2, me_h % 2
-    me_z, me_x = me_s // nx, me_s % nx
+    y, core = me_h >> 1, me_h & 1
+    me_z, me_x = me_s >> log2(nx), me_s & (nx - 1)
 
     def wrap_y(v):
-        return lax.rem(v + 2 * ny, ny)
+        return v & (ny - 1)
+
+    far_first = sorted(range(1, ny), key=lambda d: -min(d, ny - d))
 
     def on_ring(v):
         return (me_s, wrap_y(v) * 2 + core)
@@ -71,6 +73,14 @@
         return pltpu.make_async_remote_copy(
             src_ref=src, dst_ref=dst, send_sem=ssem, recv_sem=rsem, device_id=to, device_id_type=MESH
         )
+
+    def peer_of(n, sign):
+        j = n >> log2(KEEP)
+        m = j >> log2(nx)
+        mag = (nz - m) >> 1
+        dz = mag * (1 - 2 * (m & 1))
+        dx = (nx - 1) - (j & (nx - 1))
+        return (((me_z + sign * dz) & (nz - 1)) << log2(nx)) + ((me_x + sign * dx) & (nx - 1))
 
     loads = [
         (slot_hbm, slot_row), (offset_hbm, offset_row), (q_hbm, q_v), (k_hbm, k_v), (v_hbm, v_v),
@@ -82,23 +92,15 @@
 
     barrier = pltpu.get_barrier_semaphore()
 
-    @pl.loop(1, n_seq)
-    def _(i):
+    @pl.loop(0, n_seq - 1)
+    def _(j):
         pl.semaphore_signal(
-            barrier, inc=1, device_id=(lax.rem(me_s + i, n_seq), me_h), device_id_type=MESH
+            barrier, inc=1, device_id=(peer_of(j << log2(KEEP), 1), me_h), device_id_type=MESH
         )
 
     for d in range(1, ny):
         pl.semaphore_signal(barrier, inc=1, device_id=on_ring(y + d), device_id_type=MESH)
     pl.semaphore_signal(barrier, inc=1, device_id=sibling, device_id_type=MESH)
-
-    def peer_of(n, sign):
-        j = n >> log2(KEEP)
-        m = j >> log2(nx)
-        mag = (nz - m) >> 1
-        dz = jnp.where((m & 1) == 0, mag, -mag)
-        dx = (nx - 1) - (j & (nx - 1))
-        return (((me_z + sign * dz) & (nz - 1)) << log2(nx)) + ((me_x + sign * dx) & (nx - 1))
 
     def first_position(start):
         return start + ((me_s - start) & (n_seq - 1))
@@ -115,16 +117,6 @@
         return ((peer_of(n, 1) - my_start) & (n_seq - 1)) + n_seq * (n & (KEEP - 1))
 
     order = one_hot(col_q == token_of(n_q))
-    side = PACK * nj
-    row_p = lax.broadcasted_iota(jnp.int32, (side, side), 0)
-    col_p = lax.broadcasted_iota(jnp.int32, (side, side), 1)
-
-    def packed_from(q):
-        return ((q >> log2(KEEP)) & (FEAT // 128 - 1)) * rc + (q >> log2(PACK)) * KEEP + (q & (KEEP - 1))
-
-    pack_m[...] = one_hot(col_p == packed_from(row_p))
-    unpack_m[...] = one_hot(row_p == packed_from(col_p))
-
     copies[2].wait()
     qp[...] = dot(order, q_v[...]).astype(BF16)
     copies[3].wait()
@@ -198,13 +190,6 @@
             def _():
                 op(way)
 
-    def peer_scalar(j):
-        m = j // nx
-        mag = (nz - m) // 2
-        dz = jnp.where(m % 2 == 0, mag, -mag)
-        dx = (nx - 1) - j % nx
-        return lax.rem(me_z + dz + nz, nz) * nx + lax.rem(me_x + dx, nx)
-
     def send_chunk(r):
         sib_arrival(r, hops).wait_recv()
         o = origin_of(hops)
@@ -212,6 +197,11 @@
         lhs = jnp.concatenate([att[o, i, rows, :] for i in range(2 * HEADS)], axis=1)
         total = (acc[rows, :] + dot(lhs, weights_of(o))).astype(BF16)
         src_tok[rows, :] = total
+        for g in (0, 1):
+            @pl.when(r == 2 * g + 1)
+            def _():
+                img_partial(g)
+
         stacked = jnp.concatenate(
             [total[:, f * 128:(f + 1) * 128] for f in range(FEAT // 128)], axis=0
         )
@@ -222,11 +212,16 @@
         def _():
             recv_b[chunks - 1, nj - 1] = send_b[chunks - 1, nj - 1]
 
-        @pl.loop(0, nj - jnp.where(r == chunks - 1, 1, 0))
+        @pl.when(r < chunks // 2)
+        def _():
+            start_sends(r, nj)
+
+    def start_sends(r, count):
+        @pl.loop(0, count)
         def _(jj):
             remote(
                 send_b.at[r, jj], recv_b.at[r, jj], a2a_send.at[r], a2a_recv.at[r],
-                (peer_scalar(r * nj + jj), me_h),
+                (peer_of((r * nj + jj) << log2(KEEP), 1), me_h),
             ).start()
 
     def a2a_all(r):
@@ -283,7 +278,7 @@
         lane = lax.broadcasted_iota(jnp.int32, (img_tok, 128), 1)
         rs_send[:, :KV_HD] = chip[:, :KV_HD].astype(BF16)
         rs_send[:, KV_HD:] = jnp.where(lane < 64, high, low).astype(BF16)
-        for d in range(1, ny):
+        for d in far_first:
             text_rs(d).start()
 
     def text_rows_of(o):
@@ -315,7 +310,7 @@
         first, second = projected[:, :128], projected[:, 128:]
         kvfin[core, text_rows_of(y), :128] = (first * trig[0] - second * trig[1]).astype(BF16)
         kvfin[core, text_rows_of(y), 128:] = (second * trig[0] + first * trig[1]).astype(BF16)
-        for d in range(1, ny):
+        for d in far_first:
             text_ag(d).start()
 
     def text_forward():
@@ -341,7 +336,7 @@
         high, low = two_parts(chip[:, KV:].reshape(ny, mine_rows, 128))
         img_rs[g, :, :, :KV_HD] = jnp.concatenate([sums[:, :, :KV_HD], sums[:, :, KV_HD:]], axis=1).astype(BF16)
         img_rs[g, :, :, KV_HD:] = jnp.concatenate([high, low], axis=1).astype(BF16)
-        for d in range(1, ny):
+        for d in far_first:
             remote(
                 img_rs.at[g, wrap_y(y + d)], img_rr.at[g, d - 1], rs_ssem.at[1 + g], rs_rsem.at[1 + g],
                 on_ring(y + d),
@@ -375,7 +370,7 @@
             def go():
                 j = (2 * g + core) * nj + 2 * y + one
                 remote(
-                    kvs.at[g, one], kvr.at[core, y, g, one], kva_send.at[g], kva_recv.at[g], (peer_scalar(j), me_h)
+                    kvs.at[g, one], kvr.at[core, y, g, one], kva_send.at[g], kva_recv.at[g], (peer_of(j << log2(KEEP), 1), me_h)
                 ).start()
 
             if g == 1 and one == 1:
@@ -400,8 +395,9 @@
             pl.when(keeps_own)(lambda: all_of(1))
             pl.when(jnp.logical_not(keeps_own))(lambda: all_of(2))
 
-    def img_ag(d):
-        return remote(kvr.at[core, y], kvr.at[core, y], ag_ssem.at[1], ag_rsem.at[1, d - 1], on_ring(y + d))
+    def img_ag(d, g):
+        block = kvr.at[core, y, g]
+        return remote(block, block, ag_ssem.at[1], ag_rsem.at[1, d - 1], on_ring(y + d))
 
     def img_ag_arrival(d):
         block = kvr.at[core, wrap_y(y - d)]
@@ -411,11 +407,25 @@
         block = kvr.at[core, pl.ds(0, ny - 1)]
         return remote(block, block, ag_ssem.at[1], ag_rsem.at[1, 0], sibling)
 
+    def img_fwd_from(o):
+        block = kvr.at[core, o]
+        return remote(block, block, fwd_send.at[1], fwd_recv.at[1], sibling)
+
     def img_fwd(side_core):
         block = kvr.at[side_core]
         return remote(block, block, fwd_send.at[1], fwd_recv.at[1], sibling)
 
     def prepare():
+        side = PACK * nj
+        row_p = lax.broadcasted_iota(jnp.int32, (side, side), 0)
+        col_p = lax.broadcasted_iota(jnp.int32, (side, side), 1)
+
+        def packed_from(q):
+            return ((q >> log2(KEEP)) & (FEAT // 128 - 1)) * rc + (q >> log2(PACK)) * KEEP + (q & (KEEP - 1))
+
+        pack_m[...] = one_hot(col_p == packed_from(row_p))
+        unpack_m[...] = one_hot(row_p == packed_from(col_p))
+
         n_lane = lax.broadcasted_iota(jnp.int32, (n_seq, img_tok), 1)
         i_sub = lax.broadcasted_iota(jnp.int32, (n_seq, img_tok), 0)
         square_s = lax.broadcasted_iota(jnp.int32, (n_seq, n_seq), 0)
@@ -458,11 +468,15 @@
         row = e * per_example + m
         return jnp.where(row >= first, row + KEEP, row)
 
+    attend(0)
     pl.semaphore_wait(barrier, n_seq - 1 + ny)
 
     @pl.loop(0, chunks)
     def _(r):
-        attend(r)
+        @pl.when(r > 0)
+        def _():
+            attend(r)
+
         if hops > 1:
             ring_copy(r, 0, 1).start()
             ring_copy(r, 1, 1).start()
@@ -506,40 +520,52 @@
         def _():
             send_chunk(r - 1)
 
-        for g in (0, 1):
-            @pl.when(r == 2 * g + 2)
-            def _():
-                img_partial(g)
-
-    img_scatter(0)
+        @pl.when(r == 3)
+        def _():
+            img_scatter(0)
+
     img_scatter(1)
-    text_finish()
     img_finish(0)
     img_finish(1)
-    text_forward()
-    for r in range(chunks):
-        take_chunk(r)
+    for r in range(chunks // 2, chunks):
+        start_sends(r, nj - 1 if r == chunks - 1 else nj)
+    text_finish()
     hot = one_hot(lax.broadcasted_iota(jnp.int32, (local_rows, img_tok), 0) == place[:, img_tok:])
     is_image = jnp.sum(hot.astype(F32), axis=1, keepdims=True)
+    for r in range(chunks // 2):
+        take_chunk(r)
     for g in (0, 1):
         kva_each(g, lambda c: c.wait_recv())
-    for d in range(1, ny):
-        img_ag(d).start()
+        for d in far_first:
+            img_ag(d, g).start()
+    for r in range(chunks // 2, chunks):
+        take_chunk(r)
+    text_forward()
     merged_v[...] = jnp.where(is_image > 0.5, dot(hot, tok[...]), text_v[...].astype(F32)).astype(BF16)
     merged_out = pltpu.make_async_copy(merged_v, merged_hbm, out_sem.at[0])
     merged_out.start()
     text_fwd(1 - core).wait_recv()
     hot_text = one_hot(lax.broadcasted_iota(jnp.int32, (local_rows, img_tok), 0) == place[:, :img_tok])
     kv_acc[...] = dot(hot_text, jnp.concatenate([kvfin[0], kvfin[1]], axis=1))
-    for d in range(1, ny):
+    img_fwd_from(y).start()
+    for d in reversed(far_first):
         img_ag_arrival(d).wait_recv()
-    img_fwd(core).start()
+        img_fwd_from(wrap_y(y - d)).start()
+
+    def unpack_kv(side_core):
+        for g in (0, 1):
+            rows = pl.ds(pl.multiple_of((2 * g + side_core) * rc, rc), rc)
+            kv_img[rows, :] = unpack(kvr[side_core, :, g].reshape(nj * PACK, 128))
+
+    unpack_kv(core)
     img_fwd(1 - core).wait_recv()
-    for r in range(chunks):
-        kv_img[r * rc:(r + 1) * rc, :] = unpack(kvr[r % 2, :, r // 2].reshape(nj * PACK, 128))
-    kv_v[...] = (kv_acc[...] + dot(hot, kv_img[...])).astype(BF16)
-    kv_out = pltpu.make_async_copy(kv_v, kv_hbm, out_sem.at[1])
-    kv_out.start()
+    unpack_kv(1 - core)
+    kv_out = []
+    for half in (0, 1):
+        rows = slice(half * local_rows // 2, (half + 1) * local_rows // 2)
+        kv_v[rows, :] = (kv_acc[rows, :] + dot(hot[rows], kv_img[...])).astype(BF16)
+        kv_out.append(pltpu.make_async_copy(kv_v.at[rows], kv_hbm.at[rows], out_sem.at[1 + half]))
+        kv_out[half].start()
 
     for way in (0, 1):
         for hop in range(1, hops + 1):
@@ -561,7 +587,8 @@
     img_ag_all().wait_send()
     img_fwd(core).wait_send()
     merged_out.wait()
-    kv_out.wait()
+    kv_out[0].wait()
+    kv_out[1].wait()
 
 
 def on_device(
@@ -638,7 +665,7 @@
             pltpu.VMEM((local_rows, KV), BF16),
             pltpu.VMEM((local_rows, KV), F32),
             dma((10,)),
-            dma((2,)),
+            dma((3,)),
             dma((2, hops)),
             dma((chunks, 2, hops)),
             dma((2 * hops,)),

time: 77 us -> 73.8 us (0.958)
  Pallas kernels: 72.4 us -> 69.2 us
    pallas_call x1, Pallas kernels: 72.4 us -> 69.2 us  [on_device(): pl.pallas_call(functools.partial(kernel, sizes), out_shape=(jax.ShapeDtyp...]
where the time goes in v3:
time: 73.8 us; the launch traced here: 73.6 us
  Pallas kernels  69.2 us (94%)
  local copies, waits for them, and re-layouts  3.74 us (5%)
    pallas_call x1, Pallas kernels, on_device(): pl.pallas_call(functools.partial(kernel, sizes), out_shape=(jax.ShapeDtyp...  69.2 us
    unnamed x2, local copies, waits for them, and re-layouts  3.74 us

profile of v3, /device:TPU:1, one launch (start us, length us, event | category | flops | bytes accessed | tf_op | source)
XLA Modules:
  0.0 73.6 jit_solution(13342927854973960134)
XLA Ops:
  0.6 69.2 %shard_map.113 = (bf16[512,512]{1,0:T(8,128)(2,1)}, bf16[512,512]{1,0:T(8,128)(2,1)}) custom-call(bf16[256,384]{1,0:T(8,128)(2,1)} %q_hbm.1, bf16[256,384]{1,0:T(8,128)(2,1)} %k_hbm.1, bf16[256,384]{1,0:T(8,128)(2,1)} %v_hbm.1, bf16[6144,512]{1,0:T(8,128)(2,1)} %w_hbm.1, bf16[512,512]{1,0:T(8,128)(2,1)} %bitcast.6, bf16[512,512]{1,0:T(8,128)(2,1)} %kvw_hbm.1, ...), custom_call_target="tpu_custom_call" | custom-call | flops 2000000000 | bytes 10000000 | tf_op jit(solution)/shard_map/pallas_call | solution.py:620
  69.8 1.9 %copy.14 = bf16[512,1,512]{2,0,1:T(8,128)(2,1)} copy(bf16[512,1,512]{2,0,1:T(8,128)(2,1)} %bitcast.8) | data formatting | bytes 1048576
  71.7 1.9 %copy.15 = bf16[512,1,512]{2,0,1:T(8,128)(2,1)} copy(bf16[512,1,512]{2,0,1:T(8,128)(2,1)} %bitcast.7) | data formatting | bytes 1048576
